TPU v7x, 512 devices: a whole 4x8x8 slice. The times are simulated.
512 devices in a mesh: ctx: 32 (over x, y), rep: 8 (over z), fsdp: 2 (over core).
Axes of the slice: x: 4, y: 8, z: 8, core: 2. Of those that a mesh axis runs over, the one named last changes fastest.
Arguments:
- values: bfloat16 [8, 4096, 2048], P('rep', 'ctx', 'fsdp'), may hold values from -6 to 6
- gates: bfloat16 [8, 4096, 2048], P('rep', 'ctx', 'fsdp'), may hold values from -6 to 6
- skip_gain: float32 [2048], P('fsdp'), may hold values from -4 to 4
- filter_taps: float32 [4096, 2048], P('ctx', 'fsdp'), may hold values from -8 to 8
- out_weight: bfloat16 [2048, 4096], P('fsdp', 'rep'), may hold values from -0.125 to 0.125
Outputs:
- output: bfloat16 [8, 4096, 4096], P(None, 'ctx', ('rep', 'fsdp'))
All inputs are finite; a program needn't handle non-finite values.
Results may differ from a plain program's by a relative error of at most 0.0049.
Values may be sent and summed in bfloat16 or wider, within the bound.
No kernel may reach another device: no remote copies, remote signals or barrier semaphores. Data moves between devices by JAX's collectives and lax.ppermute only.
A program may use at most 128 MiB of HBM per device.

v0:
```python
import math

import jax
import jax.numpy as jnp
from jax import lax
from jax.sharding import PartitionSpec as P


def passed_along(block, axis, distance):
    devices = range(lax.axis_size(axis))
    route = [(i - distance, i) for i in devices if i - distance in devices]
    return lax.ppermute(block, axis, route)


def exact_dot(left, right):
    return jnp.dot(left, right, precision=lax.Precision.HIGHEST, preferred_element_type=jnp.float32)


def dft_tables(block):
    points = 2 * block
    freq_col = jnp.arange(block + 1, dtype=jnp.int32)[:, None]
    time_row = jnp.arange(block, dtype=jnp.int32)[None, :]
    phase = 2.0 * math.pi / points * (freq_col * time_row % points).astype(jnp.float32)
    fwd_cos = jnp.cos(phase)
    fwd_sin = -jnp.sin(phase)
    out_col = jnp.arange(points, dtype=jnp.int32)[:, None]
    freq_row = jnp.arange(block + 1, dtype=jnp.int32)[None, :]
    inv_phase = 2.0 * math.pi / points * (out_col * freq_row % points).astype(jnp.float32)
    weights = (
        jnp.where((freq_row == 0) | (freq_row == block), 1.0, 2.0).astype(jnp.float32) / points
    )
    inv_cos = weights * jnp.cos(inv_phase)
    inv_sin = -weights * jnp.sin(inv_phase)
    return (fwd_cos, fwd_sin, inv_cos, inv_sin)


def block_conv(stacked, taps, tables):
    fwd_cos, fwd_sin, inv_cos, inv_sin = tables
    seqs, block, width = stacked.shape
    freqs = block + 1
    cols_in = stacked.transpose(1, 0, 2).reshape(block, seqs * width)
    all_taps = lax.all_gather(taps, "ctx", axis=0, tiled=True)
    count = all_taps.shape[0] // block
    tap_blocks = all_taps.reshape(count, block, width)
    taps_real = jnp.einsum("ft,ktc->kfc", fwd_cos, tap_blocks, precision=lax.Precision.HIGHEST)
    taps_imag = jnp.einsum("ft,ktc->kfc", fwd_sin, tap_blocks, precision=lax.Precision.HIGHEST)
    mine = lax.axis_index("ctx")
    empty = jnp.zeros((freqs, seqs, width), jnp.float32)
    piece = lax.all_gather(cols_in, "ctx", axis=0, tiled=True)
    blocks_in = piece.shape[0] // block
    group = 4
    turns = blocks_in // group
    within = jnp.arange(group, dtype=jnp.int32)

    def add_group(step, totals):
        rows = lax.dynamic_slice_in_dim(piece, step * group * block, group * block, 0)
        rows = rows.reshape(group, block, seqs * width).astype(jnp.float32)
        src_real = jnp.einsum("ft,gtn->gfn", fwd_cos, rows, precision=lax.Precision.HIGH).reshape(
            group, freqs, seqs, width
        )
        src_imag = jnp.einsum("ft,gtn->gfn", fwd_sin, rows, precision=lax.Precision.HIGH).reshape(
            group, freqs, seqs, width
        )
        sources = step * group + within
        lag_block = mine - sources
        live = (lag_block >= 0).astype(jnp.float32)[:, None, None]
        picked = jnp.clip(lag_block, 0, count - 1)
        lag_real = taps_real[picked] * live
        lag_imag = taps_imag[picked] * live
        total_real, total_imag = totals
        total_real = (
            total_real
            + jnp.einsum("gfsw,gfw->fsw", src_real, lag_real)
            - jnp.einsum("gfsw,gfw->fsw", src_imag, lag_imag)
        )
        total_imag = (
            total_imag
            + jnp.einsum("gfsw,gfw->fsw", src_real, lag_imag)
            + jnp.einsum("gfsw,gfw->fsw", src_imag, lag_real)
        )
        return (total_real, total_imag)

    spec_real, spec_imag = lax.fori_loop(0, turns, add_group, (empty, empty))
    wide = exact_dot(inv_cos, spec_real.reshape(freqs, seqs * width)) + exact_dot(
        inv_sin, spec_imag.reshape(freqs, seqs * width)
    )
    head = wide[:block]
    carried = passed_along(wide[block:], "ctx", 1)
    return (head + carried).reshape(block, seqs, width).transpose(1, 0, 2)


def body(values, gates, skip_gain, filter_taps, out_weight):
    block = values.shape[1]
    stacked, stacked_gates = (
        lax.all_to_all(values, "rep", split_axis=2, concat_axis=0, tiled=True),
        lax.all_to_all(gates, "rep", split_axis=2, concat_axis=0, tiled=True),
    )
    seqs = stacked.shape[0]
    width = stacked.shape[2]
    offset = lax.axis_index("rep") * width
    taps = lax.dynamic_slice_in_dim(filter_taps, offset, width, 1)
    gain = lax.dynamic_slice_in_dim(skip_gain, offset, width, 0)
    tables = dft_tables(block)
    convolved = block_conv(stacked, taps, tables)
    mixed = (
        stacked_gates.astype(jnp.float32)
        * (convolved + gain[None, None, :] * stacked.astype(jnp.float32))
    ).astype(jnp.bfloat16)
    piece = lax.all_gather(mixed, "rep", axis=2, tiled=True)
    rows = piece.shape[2]
    partial_out = jnp.dot(
        piece.reshape(seqs * block, rows), out_weight, preferred_element_type=jnp.float32
    )
    partial_out = partial_out.reshape(seqs, block, out_weight.shape[1])
    return lax.psum_scatter(partial_out, "fsdp", scatter_dimension=2, tiled=True).astype(
        jnp.bfloat16
    )


def solution(mesh):
    return jax.shard_map(
        body,
        mesh=mesh,
        in_specs=(
            P("rep", "ctx", "fsdp"),
            P("rep", "ctx", "fsdp"),
            P("fsdp"),
            P("ctx", "fsdp"),
            P("fsdp", "rep"),
        ),
        out_specs=P(None, "ctx", ("rep", "fsdp")),
        check_vma=False,
    )
```

profile of v0, /device:TPU:1, one launch (start us, length us, event | category | flops | bytes accessed | tf_op | source)
XLA Modules:
  0.0 510.4 jit_solution(3660814026261501577)
XLA Ops:
  12.3 21.0 %all_to_all.27 = bf16[8,2,8192]{2,1,0:T(2,128)(2,1)S(1)} all-to-all(bf16[8,2,8192]{2,1,0:T(2,128)(2,1)S(1)} %reshape.159), channel_id=1, replica_groups=mesh['ctx'=32,'rep'=8,'fsdp'=2] {'rep'}, dimensions={0} | all-to-all | bytes 524288 | tf_op jit(solution)/shard_map/all_to_all | solution.py:95
  35.6 60.0 %all-gather.4.cloned.1.call-done = f32[4096,128]{1,0:T(8,128)} async-done(((f32[128,128]{1,0:T(8,128)}), f32[4096,128]{1,0:T(8,128)}) %all-gather.4.cloned.1.call-update) | async-done | bytes 2097168 | tf_op jit(solution)/shard_map/all_gather | solution.py:42
  95.6 4.0 convolution_bitcast_fusion.2
  99.7 3.8 convolution_bitcast_fusion.3
  103.4 102.8 %all-gather.6.cloned.1.call-done = bf16[4096,1024]{0,1:T(8,128)(2,1)} async-done(((bf16[128,1024]{0,1:T(8,128)(2,1)}), bf16[4096,1024]{0,1:T(8,128)(2,1)}) %all-gather.6.cloned.1.call-update) | async-done | bytes 8388624 | tf_op jit(solution)/shard_map/all_gather | solution.py:49
  206.2 194.0 %while.18 = (s32[]{:T(128)}, f32[129,8,128]{2,1,0:T(8,128)}, f32[129,8,128]{2,1,0:T(8,128)}, s32[]{:T(128)}, f32[32,129,128]{2,1,0:T(8,128)}, /*index=5*/bf16[40...) while((s32[]{:T(128)}, f32[129,8,128]{2,1,0:T(8,128)}, ...), condition=%wide.region_1.2_spmd.clone, body=%wide.region_0.1_spmd.clone.sunk | while | flops 816701120 | bytes 57549184 | solution.py:83
  220.5 2.9 reshape.174
  223.3 4.0 multiply_reduce_fusion.5
  244.4 2.9 reshape.174
  247.3 4.0 multiply_reduce_fusion.5
  251.3 3.1 bitcast_add_fusion.4
  268.7 2.9 reshape.174
  271.6 4.0 multiply_reduce_fusion.5
  275.6 3.1 bitcast_add_fusion.4
  293.0 2.9 reshape.174
  295.9 4.0 multiply_reduce_fusion.5
  299.9 3.1 bitcast_add_fusion.4
  320.2 4.0 multiply_reduce_fusion.5
  324.2 3.1 bitcast_add_fusion.4
  341.6 2.9 reshape.174
  344.5 4.0 multiply_reduce_fusion.5
  348.5 3.1 bitcast_add_fusion.4
  368.8 4.0 multiply_reduce_fusion.5
  372.8 3.1 bitcast_add_fusion.4
  393.0 4.0 multiply_reduce_fusion.5
  397.1 3.1 bitcast_add_fusion.4
  406.5 3.3 collective-permute-start
  413.2 7.1 %all-to-all-start = ((bf16[8,2,8192]{2,1,0:T(2,128)(2,1)}), bf16[8,2,8192]{2,1,0:T(2,128)(2,1)S(1)}, u32[]{:S(2)}, u32[]{:S(2)}) async-start(bf16[8,2,8192]{2,1,0:T(2,128)(2,1)} %reshape.161), calls=%async_computation | async-start | bytes 524288 | tf_op jit(solution)/shard_map/all_to_all | solution.py:96
  421.3 8.3 %all-to-all-done = bf16[8,2,8192]{2,1,0:T(2,128)(2,1)S(1)} async-done(((bf16[8,2,8192]{2,1,0:T(2,128)(2,1)}), bf16[8,2,8192]{2,1,0:T(2,128)(2,1)S(1)}, u32[]{:S(2)}, u32[]{:S(2)}) %all-to-all-start) | async-done | bytes 262176 | tf_op jit(solution)/shard_map/all_to_all | solution.py:96
  432.0 43.9 %all-gather.8.cloned.1.call-done = bf16[8,128,1024]{2,1,0:T(8,128)(2,1)} async-done(((bf16[8,128,128]{2,1,0:T(8,128)(2,1)}), bf16[8,128,1024]{2,1,0:T(8,128)(2,1)}) %all-gather.8.cloned.1.call-update) | async-done | bytes 2097168 | tf_op jit(solution)/shard_map/all_gather | solution.py:109
  475.9 4.2 fusion.29
  480.1 21.7 %reduce-scatter.2.cloned.1.call-done = f32[8,128,256]{2,1,0:T(8,128)} async-done(((f32[8,128,512]{2,1,0:T(8,128)}), f32[8,128,256]{2,1,0:T(8,128)}) %reduce-scatter.2.cloned.1.call-update) | async-done | bytes 1048592 | tf_op jit(solution)/shard_map/reduce_scatter | solution.py:115
  (194 shorter events, 148.3 us)
Async XLA Ops:
  6.5 469.4 %copy-start = (bf16[1024,512]{1,0:T(8,128)(2,1)S(1)}, bf16[1024,512]{1,0:T(8,128)(2,1)}, u32[]{:S(2)}) copy-start(bf16[1024,512]{1,0:T(8,128)(2,1)} %param.11) | copy-start | bytes 3145732
  6.5 89.1 %all-gather.4.cloned.1.call-start = ((), (), s32[]{:S(2)}) async-start(), calls=%async_computation.3 | async-start | bytes 2162688 | tf_op jit(solution)/shard_map/all_gather | solution.py:42
  8.1 198.1 %all-gather.6.cloned.1.call-start = ((), (), s32[]{:S(2)}) async-start(), calls=%async_computation.4 | async-start | bytes 8650752 | tf_op jit(solution)/shard_map/all_gather | solution.py:49
  33.6 62.0 %copy-start.6 = (bf16[1024,1,128]{2,1,0:T(2,128)(2,1)}, bf16[1024,1,128]{2,1,0:T(2,128)(2,1)S(1)}, u32[]{:S(2)}) copy-start(bf16[1024,1,128]{2,1,0:T(2,128)(2,1)S(1)} %reshape.160) | copy-start | bytes 786436
  95.6 4.0 copy-start.3
  220.5 2.9 copy-start.1
  227.3 2.8 copy-start.5
  230.2 1.4 copy-start.4
  244.4 2.9 copy-start.1
  251.3 3.1 copy-start.5
  254.5 1.4 copy-start.4
  268.7 2.9 copy-start.1
  275.6 3.1 copy-start.5
  278.8 1.4 copy-start.4
  293.0 2.9 copy-start.1
  299.9 3.1 copy-start.5
  317.3 2.9 copy-start.1
  324.2 3.1 copy-start.5
  341.6 2.9 copy-start.1
  348.5 3.1 copy-start.5
  365.9 2.9 copy-start.1
  372.8 3.1 copy-start.5
  390.2 2.9 copy-start.1
  397.1 3.1 copy-start.5
  400.2 1.4 copy-start.10
  401.5 2.2 copy-start.9
  403.6 6.2 %copy-start.8 = (bf16[1,128,1024]{2,1,0:T(8,128)(2,1)S(1)}, bf16[1,128,1024]{2,1,0:T(8,128)(2,1)}, u32[]{:S(2)}) copy-start(bf16[1,128,1024]{2,1,0:T(8,128)(2,1)} %param.8) | copy-start | bytes 786436
  405.6 15.4 %copy-start.7 = (bf16[1024,1,128]{2,1,0:T(2,128)(2,1)S(1)}, bf16[1024,1,128]{2,1,0:T(2,128)(2,1)}, u32[]{:S(2)}) copy-start(bf16[1024,1,128]{2,1,0:T(2,128)(2,1)} %copy-done.6) | copy-start | bytes 786436
  406.5 23.6 %collective-permute-start = (f32[128,1024]{1,0:T(8,128)}, f32[128,1024]{1,0:T(8,128)}, u32[]{:S(2)}, u32[]{:S(2)}) collective-permute-start(f32[128,1024]{1,0:T(8,128)} %slice.13), channel_id=1, source_target_pairs={{0,16},{16,32},{32,48},{48,64},{64,80},{80,96},{96,112},{112,128},... | collective-permute-start | bytes 1572872 | tf_op jit(solution)/shard_map/ppermute | solution.py:12
  413.2 16.4 %all-to-all-start = ((bf16[8,2,8192]{2,1,0:T(2,128)(2,1)}), bf16[8,2,8192]{2,1,0:T(2,128)(2,1)S(1)}, u32[]{:S(2)}, u32[]{:S(2)}) async-start(bf16[8,2,8192]{2,1,0:T(2,128)(2,1)} %reshape.161), calls=%async_computation | async-start | bytes 524288 | tf_op jit(solution)/shard_map/all_to_all | solution.py:96
  420.2 55.7 %all-gather.8.cloned.1.call-start = ((), (), s32[]{:S(2)}) async-start(), calls=%async_computation.5 | async-start | bytes 2359296 | tf_op jit(solution)/shard_map/all_gather | solution.py:109
  431.9 69.8 %reduce-scatter.2.cloned.1.call-start = ((), (), s32[]{:S(2)}) async-start(), calls=%async_computation.6 | async-start | bytes 3145728 | tf_op jit(solution)/shard_map/reduce_scatter | solution.py:115
  (6 other events, 8.2 us)
Sparse Core Ops, SparseCore 0:
  10.5 85.0 all-gather.3
  98.6 107.5 all-gather.5
  432.0 43.8 all-gather.7
  480.2 21.5 reduce-scatter.1
where the time goes:
time: 512 us; the launch traced here: 510 us
  waiting for transfers between devices  237 us (46%)
  local copies, waits for them, and re-layouts  93.4 us (18%)
  other arithmetic  78 us (15%)
  matrix products  57.1 us (11%)
  blocking collectives  21 us (4%)
  between operations  13.4 us (3%)
  starting transfers between devices  10.5 us (2%)
    all_gather x1, waiting for transfers between devices, block_conv(): piece = lax.all_gather(cols_in, 'ctx', axis=0, tiled=True)  103 us
    all_gather x1, waiting for transfers between devices, block_conv(): all_taps = lax.all_gather(taps, 'ctx', axis=0, tiled=True)  60 us
    all_gather x1, waiting for transfers between devices, body(): piece = lax.all_gather(mixed, 'rep', axis=2, tiled=True)  43.9 us
    dot_general x8, other arithmetic, add_group(): jnp.einsum('gfsw,gfw->fsw', src_imag, lag_real)  32.1 us
    add x8, other arithmetic, add_group(): total_imag + jnp.einsum('gfsw,gfw->fsw', src_real, lag_imag)  24.7 us
    reshape x8, local copies, waits for them, and re-layouts, add_group(): jnp.einsum('ft,gtn->gfn', fwd_cos, rows, precision=lax.Precision.HIGH)  23 us
    reshape x8, local copies, waits for them, and re-layouts, add_group(): jnp.einsum('ft,gtn->gfn', fwd_sin, rows, precision=lax.Precision.HIGH)  22.1 us
    reduce_scatter x1, waiting for transfers between devices, body(): lax.psum_scatter(partial_out, 'fsdp', scatter_dimension=2, tiled=True)  21.7 us
  transfers between devices with their start and end apart: 6, of which 5 were waited for; matrix products, arithmetic and copies ran while one was open for 4% of the time, Pallas kernels for 0%

commit v1 on v0

v1 whole, which is shorter than its diff:
```python
import math

import jax
import jax.numpy as jnp
import ml_dtypes
import numpy as np
from jax import lax
from jax.experimental import pallas as pl
from jax.experimental.pallas import tpu as pltpu
from jax.sharding import PartitionSpec as P

F32, BF16 = jnp.float32, jnp.bfloat16


def two_parts(table):
    high = table.astype(ml_dtypes.bfloat16)
    low = (table - high.astype(np.float64)).astype(ml_dtypes.bfloat16)
    return high, low


def dft_tables(block):
    points = 2 * block
    angle = 2.0 * math.pi / points * (np.arange(block) + 0.5)[None, :] * np.arange(points)[:, None]
    forward = np.concatenate([np.cos(angle), -np.sin(angle)], axis=1)[:block]
    inverse = np.concatenate([np.cos(angle), -np.sin(angle)], axis=1).T * (2.0 / points)
    return np.concatenate(two_parts(forward), axis=0), np.stack(two_parts(inverse))


def pack_kernel(values_ref, taps_ref, out_ref):
    peers, rows, block = out_ref.shape
    width = rows // 2
    for first, source in ((0, values_ref), (width, taps_ref)):
        turned = source[...].astype(F32).T.astype(BF16)
        out_ref[:, first : first + width, :] = turned.reshape(peers, width, block)


def conv_kernel(in_ref, fwd_ref, inv_ref, out_ref, src, lag, spec):
    count, rows, block = in_ref.shape
    width = rows // 2
    for first, dest in ((0, src), (width, lag)):
        part = in_ref[:, first : first + width, :].reshape(count * width, block)
        both = jnp.concatenate([part, part], axis=1)
        wave = jnp.dot(both, fwd_ref[...], preferred_element_type=F32)
        real = wave[:, :block].reshape(count, width, block)
        imag = wave[:, block:].reshape(count, width, block)
        dest[0] = real
        dest[1] = imag
        dest[2] = real + imag

    group = 4

    def some_channels(step, carry):
        here = pl.ds(pl.multiple_of(step * 8, 8), 8)
        for i0 in range(0, count, group):
            sums = [[None] * 3 for _ in range(group)]
            for j0 in range(0, i0 + group, group):
                for p in range(3):
                    taps = {k: lag[p, k, here, :] for k in range(max(i0 - j0 - group + 1, 0), i0 - j0 + group)}
                    for dj in range(group):
                        source = src[p, j0 + dj, here, :]
                        for di in range(group):
                            k = i0 + di - j0 - dj
                            if k >= 0:
                                term = source * taps[k]
                                sums[di][p] = term if sums[di][p] is None else sums[di][p] + term
            for di in range(group):
                rr, ii, ss = sums[di]
                spec[i0 + di, here, :block] = rr - ii
                spec[i0 + di, here, block:] = ss - rr - ii
        return carry

    lax.fori_loop(0, width // 8, some_channels, 0)
    whole = spec[...].reshape(count * width, 2 * block)
    high = whole.astype(BF16)
    low = (whole - high.astype(F32)).astype(BF16)
    wide = (
        jnp.dot(high, inv_ref[0], preferred_element_type=F32)
        + jnp.dot(low, inv_ref[0], preferred_element_type=F32)
        + jnp.dot(high, inv_ref[1], preferred_element_type=F32)
    )
    head = wide[:, :block].reshape(count, width, block)
    tail = wide[:, block:].reshape(count, width, block)
    out_ref[0] = head[0].astype(BF16)
    out_ref[1:] = (head[1:] + tail[:-1]).astype(BF16)


def gate_kernel(conv_ref, values_ref, gates_ref, gain_ref, out_ref):
    peers, width, block = conv_ref.shape
    convolved = conv_ref[...].reshape(peers * width, block).astype(F32).T
    direct = gain_ref[...] * values_ref[...].astype(F32)
    out_ref[...] = (gates_ref[...].astype(F32) * (convolved + direct)).astype(BF16)


def place_kernel(place_ref, own_a, own_b, got_a, out_ref):
    mine = place_ref[0]
    seqs, block, _ = out_ref.shape
    odd = mine % 2
    even_chip = mine + odd
    odd_chip = even_chip - 1
    near_mine = jnp.where(odd == 1, odd_chip - 1, even_chip)
    near_theirs = jnp.where(odd == 1, even_chip, odd_chip - 1)
    far_mine = jnp.where(odd == 1, mine - 3, mine + 2)
    for part, first, second in (
        (own_a, near_mine, near_mine + 1),
        (got_a, near_theirs, near_theirs + 1),
        (own_b, far_mine, far_mine + 1),
    ):
        out_ref[lax.rem(first + 2 * seqs, seqs)] = part[:block]
        out_ref[lax.rem(second + 2 * seqs, seqs)] = part[block:]


def place_most(place, own_a, own_b, got_a, seqs, block):
    return pl.pallas_call(
        place_kernel,
        in_specs=[pl.BlockSpec(memory_space=pltpu.SMEM)] + [pl.BlockSpec(memory_space=pltpu.VMEM)] * 3,
        out_shape=jax.ShapeDtypeStruct((seqs, block, own_a.shape[1]), BF16),
        name="place",
    )(place, own_a, own_b, got_a)


def body(values, gates, skip_gain, filter_taps, out_weight):
    block, chans = values.shape[1:]
    peers = lax.axis_size("ctx")
    width = chans // peers
    values, gates = values[0], gates[0]
    forward, inverse = dft_tables(block)
    count = lax.axis_size("rep")
    mine, core = lax.axis_index("rep"), lax.axis_index("fsdp")
    place = jnp.stack([mine, core]).astype(jnp.int32)
    row_pairs = [[i, i + 1] for i in range(0, count, 2)]
    column_swap = [(i, (i - 1 if i % 2 == 0 else i + 1) % count) for i in range(count)]
    onward = [(i, (i - 2 if i % 2 == 0 else i + 2) % count) for i in range(count)]
    partner_weight = lax.ppermute(out_weight, "rep", column_swap)

    packed = pl.pallas_call(
        pack_kernel, out_shape=jax.ShapeDtypeStruct((peers, 2 * width, block), BF16), name="pack"
    )(values, filter_taps)
    turned = lax.all_to_all(packed, "ctx", split_axis=0, concat_axis=0, tiled=True)
    convolved = pl.pallas_call(
        conv_kernel,
        out_shape=jax.ShapeDtypeStruct((peers, width, block), BF16),
        scratch_shapes=[
            pltpu.VMEM((3, peers, width, block), F32),
            pltpu.VMEM((3, peers, width, block), F32),
            pltpu.VMEM((peers, width, 2 * block), F32),
        ],
        compiler_params=pltpu.CompilerParams(vmem_limit_bytes=40 * 2**20),
        name="conv",
    )(turned, forward, inverse)
    back = lax.all_to_all(convolved, "ctx", split_axis=0, concat_axis=0, tiled=True)
    mixed = pl.pallas_call(
        gate_kernel, out_shape=jax.ShapeDtypeStruct((block, chans), BF16), name="gate"
    )(back, values, gates, skip_gain[None, :])

    keep = out_weight.shape[1] // 2
    weights = jnp.concatenate(
        [
            lax.dynamic_slice_in_dim(w, side * keep, keep, 1)
            for side in (core, 1 - core)
            for w in (out_weight, partner_weight)
        ],
        axis=1,
    )
    near = lax.all_gather(mixed, "rep", axis=0, axis_index_groups=row_pairs)
    far = lax.ppermute(near, "rep", onward)

    def columns(product):
        came = lax.all_gather(product[:, 2 * keep :].astype(BF16), "fsdp", axis=0)
        total = product[:, : 2 * keep] + lax.dynamic_index_in_dim(came, 1 - core, 0, False).astype(F32)
        total = total.astype(BF16)
        return total[:, :keep], lax.ppermute(total[:, keep:], "rep", column_swap)

    own_a, got_a = columns(
        jnp.dot(near.reshape(2 * block, chans), weights, preferred_element_type=F32)
    )
    far, own_a = lax.optimization_barrier((far, own_a))
    own_b, got_b = columns(
        jnp.dot(far.reshape(2 * block, chans), weights, preferred_element_type=F32)
    )
    out = place_most(place, own_a, own_b, got_a, count, block)
    low = jnp.where(mine % 2 == 1, mine + 3, mine - 4 + count) % count
    return lax.dynamic_update_slice(out, got_b.reshape(2, block, keep), (low, 0, 0))


def solution(mesh):
    return jax.shard_map(
        body,
        mesh=mesh,
        in_specs=(
            P("rep", "ctx", "fsdp"),
            P("rep", "ctx", "fsdp"),
            P("fsdp"),
            P("ctx", "fsdp"),
            P("fsdp", "rep"),
        ),
        out_specs=P(None, "ctx", ("rep", "fsdp")),
        check_vma=False,
    )
```

time: 512 us -> 96 us (0.19)
  waiting for transfers between devices: 237 us -> 13.5 us
  local copies, waits for them, and re-layouts: 93.4 us -> 3.58 us
  other arithmetic: 78 us -> 0.8 us
  matrix products: 57.1 us -> 1.42 us
  starting transfers between devices: 10.5 us -> 45.5 us
  between operations: 13.4 us -> 0.17 us
  Pallas kernels: 0 us -> 11.8 us
    all_gather x3 -> x0, waiting for transfers between devices: 207 us -> none  [the longest x1 103 us: block_conv(): piece = lax.all_gather(cols_in, 'ctx', axis=0, tiled=True)]
    dot_general x21 -> x2, matrix products: 57.1 us -> 1.42 us  [the longest x1 0.71 us: body(): jnp.dot(near.reshape(2 * block, chans), weights, preferred_element_type=F32)]
    reshape x16 -> x0, local copies, waits for them, and re-layouts: 45 us -> none  [the longest x8 23 us: add_group(): jnp.einsum('ft,gtn->gfn', fwd_cos, rows, precision=lax.Precision.HIGH)]
    dot_general x8 -> x0, other arithmetic: 32.1 us -> none  [add_group(): jnp.einsum('gfsw,gfw->fsw', src_imag, lag_real)]
    add x8 -> x0, other arithmetic: 24.7 us -> none  [add_group(): total_imag + jnp.einsum('gfsw,gfw->fsw', src_real, lag_imag)]
    ppermute x1 -> x4, starting transfers between devices: 3.29 us -> 27.5 us  [the longest x1 10.7 us: body(): partner_weight = lax.ppermute(out_weight, 'rep', column_swap)]
    gather x16 -> x0, local copies, waits for them, and re-layouts: 24 us -> none  [the longest x8 18.5 us: add_group(): lag_real = taps_real[picked] * live]
    reduce_scatter x1 -> x0, waiting for transfers between devices: 21.7 us -> none  [body(): lax.psum_scatter(partial_out, 'fsdp', scatter_dimension=2, tiled=True)]
  transfers between devices with their start and end apart: 6 -> 6, of which waited for: 5 -> 4; matrix products, arithmetic and copies ran while one was open for 4% -> 4% of each run, Pallas kernels for 0% -> 8%
where the time goes in v1:
time: 96 us; the launch traced here: 94.8 us
  starting transfers between devices  45.5 us (47%)
  blocking collectives  18 us (19%)
  waiting for transfers between devices  13.5 us (14%)
  Pallas kernels  11.8 us (12%)
  local copies, waits for them, and re-layouts  3.58 us (4%)
  matrix products  1.42 us (1%)
    all_gather x2, blocking collectives, columns(): came = lax.all_gather(product[:, 2 * keep:].astype(BF16), 'fsdp', axis=0)  11.3 us
    ppermute x1, starting transfers between devices, body(): partner_weight = lax.ppermute(out_weight, 'rep', column_swap)  10.7 us
    all_to_all x1, starting transfers between devices, body(): lax.all_to_all(packed, 'ctx', split_axis=0, concat_axis=0, tiled=True)  10.5 us
    ppermute x1, starting transfers between devices, body(): far = lax.ppermute(near, 'rep', onward)  9.97 us
    all_to_all x1, starting transfers between devices, body(): lax.all_to_all(convolved, 'ctx', split_axis=0, concat_axis=0, tiled=True)  7.5 us
    ppermute x2, starting transfers between devices, columns(): return (total[:, :keep], lax.ppermute(total[:, keep:], 'rep', column_swap))  6.9 us
    all_gather x1, blocking collectives, body(): near = lax.all_gather(mixed, 'rep', axis=0, axis_index_groups=row_pairs)  6.73 us
    pallas_call x1, Pallas kernels, body(): pl.pallas_call(conv_kernel, out_shape=jax.ShapeDtypeStruct((peers, width,...  5.74 us
  transfers between devices with their start and end apart: 6, of which 4 were waited for; matrix products, arithmetic and copies ran while one was open for 4% of the time, Pallas kernels for 8%

profile of v1, /device:TPU:1, one launch (start us, length us, event | category | flops | bytes accessed | tf_op | source)
XLA Modules:
  0.0 94.8 jit_solution(9846582464455823908)
XLA Ops:
  0.0 2.2 %pack.1 = bf16[32,64,128]{2,1,0:T(8,128)(2,1)} custom-call(bf16[128,1024]{1,0:T(8,128)(2,1)} %bitcast.20, f32[128,1024]{1,0:T(8,128)} %taps_ref.1), custom_call_target="tpu_custom_call" | custom-call | tf_op jit(solution)/shard_map/pack/pallas_call | solution.py:135
  2.2 10.5 %all-to-all-start = ((bf16[32,64,128]{2,1,0:T(8,128)(2,1)}), bf16[32,64,128]{2,1,0:T(8,128)(2,1)S(1)}, u32[]{:S(2)}, u32[]{:S(2)}) async-start(bf16[32,64,128]{2,1,0:T(8,128)(2,1)} %pack.1), calls=%async_computation | async-start | bytes 1048576 | tf_op jit(solution)/shard_map/all_to_all | solution.py:138
  12.8 10.7 %collective-permute-start.1 = (bf16[1024,512]{1,0:T(8,128)(2,1)S(1)}, bf16[1024,512]{1,0:T(8,128)(2,1)S(1)}, u32[]{:S(2)}, u32[]{:S(2)}) collective-permute-start(bf16[1024,512]{1,0:T(8,128)(2,1)S(1)} %copy-done.2), channel_id=1, source_target_pairs={{0,14},{2,4},{4,2},{6,8},{8,6},{10,12},{12,10},{14,0},{1,15},{3,5}... | collective-permute-start | bytes 3145736 | tf_op jit(solution)/shard_map/ppermute | solution.py:133
  23.4 3.6 %all-to-all-done.in_ref = bf16[32,64,128]{2,1,0:T(8,128)(2,1)S(1)} async-done(((bf16[32,64,128]{2,1,0:T(8,128)(2,1)}), bf16[32,64,128]{2,1,0:T(8,128)(2,1)S(1)}, u32[]{:S(2)}, u32[]{:S(2)}) %all-to-all-start) | async-done | bytes 524320 | tf_op jit(solution)/shard_map/all_to_all | solution.py:138
  27.1 0.0 copy-done.1
  27.1 5.7 %conv.1 = bf16[32,32,128]{2,1,0:T(8,128)(2,1)} custom-call(bf16[32,64,128]{2,1,0:T(8,128)(2,1)S(1)} %all-to-all-done.in_ref, bf16[256,256]{1,0:T(8,128)(2,1)S(1)} %copy-done.1, bf16[2,256,256]{2,1,0:T(8,128)(2,1)S(1)} %copy-done), custom_call_target="tpu_custom_call" | custom-call | tf_op jit(solution)/shard_map/conv/pallas_call | solution.py:139
  32.8 7.5 %all-to-all-start.1 = ((bf16[32,32,128]{2,1,0:T(8,128)(2,1)}), bf16[32,32,128]{2,1,0:T(8,128)(2,1)S(1)}, u32[]{:S(2)}, u32[]{:S(2)}) async-start(bf16[32,32,128]{2,1,0:T(8,128)(2,1)} %conv.1), calls=%async_computation.1 | async-start | bytes 524288 | tf_op jit(solution)/shard_map/all_to_all | solution.py:150
  40.3 0.1 constant_dynamic-slice_fusion.3
  40.4 5.6 %collective-permute-done.1 = bf16[1024,512]{1,0:T(8,128)(2,1)S(1)} collective-permute-done((bf16[1024,512]{1,0:T(8,128)(2,1)S(1)}, bf16[1024,512]{1,0:T(8,128)(2,1)S(1)}, u32[]{:S(2)}, u32[]{:S(2)}) %collective-permute-start.1) | collective-permute-done | bytes 1048608 | tf_op jit(solution)/shard_map/ppermute | solution.py:133
  46.0 0.1 constant_dynamic-slice_fusion.2
  46.1 3.9 %all-to-all-done.1.conv_ref = bf16[32,32,128]{2,1,0:T(8,128)(2,1)S(1)} async-done(((bf16[32,32,128]{2,1,0:T(8,128)(2,1)}), bf16[32,32,128]{2,1,0:T(8,128)(2,1)S(1)}, u32[]{:S(2)}, u32[]{:S(2)}) %all-to-all-start.1) | async-done | bytes 262176 | tf_op jit(solution)/shard_map/all_to_all | solution.py:150
  50.0 0.7 copy-done.3
  50.7 1.9 %gate.1 = bf16[128,1024]{1,0:T(8,128)(2,1)} custom-call(bf16[32,32,128]{2,1,0:T(8,128)(2,1)} %copy-done.3, bf16[128,1024]{1,0:T(8,128)(2,1)} %bitcast.21, bf16[128,1024]{1,0:T(8,128)(2,1)} %bitcast.23, f32[1,1024]{1,0:T(1,128)} %bitcast.25), custom_call_target="tpu_custom_call" | custom-call | tf_op jit(solution)/shard_map/gate/pallas_call | solution.py:151
  52.6 6.7 %all-gather = bf16[256,1024]{1,0:T(8,128)(2,1)S(1)} all-gather(bf16[128,1024]{1,0:T(8,128)(2,1)} %gate.1), channel_id=2, replica_groups={{0,2},{4,6},{8,10},{12,14},{1,3},{5,7},{9,11},{13,15},{16,18},{20,22},{..., dimensions={0}, use_global_device_ids=true | all-gather | bytes 786432 | tf_op jit(solution)/shard_map/all_gather | solution.py:164
  59.4 10.0 %collective-permute-start = (bf16[2,128,1024]{2,1,0:T(8,128)(2,1)S(1)}, bf16[2,128,1024]{2,1,0:T(8,128)(2,1)S(1)}, u32[]{:S(2)}, u32[]{:S(2)}) collective-permute-start(bf16[2,128,1024]{2,1,0:T(8,128)(2,1)S(1)} %bitcast.22), channel_id=1, source_target_pairs={{0,12},{2,6},{4,0},{6,10},{8,4},{10,14},{12,8},{14,2},{1,13},{3,7}... | collective-permute-start | bytes 1572872 | tf_op jit(solution)/shard_map/ppermute | solution.py:165
  69.3 0.7 fusion.3
  70.1 6.9 %all-gather.1 = bf16[512,512]{1,0:T(8,128)(2,1)S(1)} all-gather(bf16[256,512]{1,0:T(8,128)(2,1)S(1)} %slice.51), channel_id=3, replica_groups=mesh['ctx'=32,'rep'=8,'fsdp'=2] {'fsdp'}, dimensions={0}, use_global_device_ids=true | all-gather | bytes 786432 | tf_op jit(solution)/shard_map/all_gather | solution.py:168
  77.0 0.1 fusion.1
  77.1 0.7 fusion.7
  77.8 1.9 %collective-permute-start.2 = (bf16[256,256]{1,0:T(8,128)(2,1)S(1)}, bf16[256,256]{1,0:T(8,128)(2,1)S(1)}, u32[]{:S(2)}, u32[]{:S(2)}) collective-permute-start(bf16[256,256]{1,0:T(8,128)(2,1)S(1)} %get-tuple-element.15), channel_id=1, source_target_pairs={{0,14},{2,4},{4,2},{6,8},{8,6},{10,12},{12,10},{14,0},{1,15},{3,5}... | collective-permute-start | bytes 393224 | tf_op jit(solution)/shard_map/ppermute | solution.py:171
  79.7 0.0 collective-permute-done
  79.7 0.7 fusion.2
  80.5 4.4 %all-gather.2 = bf16[512,512]{1,0:T(8,128)(2,1)S(1)} all-gather(bf16[256,512]{1,0:T(8,128)(2,1)S(1)} %slice.50), channel_id=4, replica_groups=mesh['ctx'=32,'rep'=8,'fsdp'=2] {'fsdp'}, dimensions={0}, use_global_device_ids=true | all-gather | bytes 786432 | tf_op jit(solution)/shard_map/all_gather | solution.py:168
  84.8 0.1 fusion
  84.9 0.7 fusion.6
  85.6 5.0 %collective-permute-start.3 = (bf16[256,256]{1,0:T(8,128)(2,1)S(1)}, bf16[256,256]{1,0:T(8,128)(2,1)S(1)}, u32[]{:S(2)}, u32[]{:S(2)}) collective-permute-start(bf16[256,256]{1,0:T(8,128)(2,1)S(1)} %get-tuple-element.13), channel_id=1, source_target_pairs={{0,14},{2,4},{4,2},{6,8},{8,6},{10,12},{12,10},{14,0},{1,15},{3,5}... | collective-permute-start | bytes 393224 | tf_op jit(solution)/shard_map/ppermute | solution.py:171
  90.6 0.6 pad_add_fusion.place_ref
  91.2 0.0 collective-permute-done.2.got_a
  91.2 0.7 copy-done.4
  91.9 1.9 %place.1 = bf16[8,128,256]{2,1,0:T(8,128)(2,1)} custom-call(s32[2]{0:T(128)} %pad_add_fusion.place_ref, bf16[256,256]{1,0:T(8,128)(2,1)} %get-tuple-element.7.own_a, bf16[256,256]{1,0:T(8,128)(2,1)} %get-tuple-element.14.own_b, bf16[256,256]{1,0:T(8,128)(2,1)} %copy-done.4), custom_call_target="tpu_custom_call" | custom-call | tf_op jit(solution)/shard_map/place/pallas_call | solution.py:113
  93.8 0.4 collective-permute-done.3
  94.1 0.7 constant_dynamic-update-slice_fusion
  (9 shorter events, 0.1 us)
Async XLA Ops:
  0.0 12.8 %copy-start.2 = (bf16[1024,512]{1,0:T(8,128)(2,1)S(1)}, bf16[1024,512]{1,0:T(8,128)(2,1)}, u32[]{:S(2)}) copy-start(bf16[1024,512]{1,0:T(8,128)(2,1)} %param.11) | copy-start | bytes 3145732
  0.0 27.1 %copy-start = (bf16[2,256,256]{2,1,0:T(8,128)(2,1)S(1)}, bf16[2,256,256]{2,1,0:T(8,128)(2,1)}, u32[]{:S(2)}) copy-start(bf16[2,256,256]{2,1,0:T(8,128)(2,1)} %constant.55.clone.inv_ref) | copy-start | bytes 786436
  0.0 27.1 %copy-start.1 = (bf16[256,256]{1,0:T(8,128)(2,1)S(1)}, bf16[256,256]{1,0:T(8,128)(2,1)}, u32[]{:S(2)}) copy-start(bf16[256,256]{1,0:T(8,128)(2,1)} %constant.54.clone.fwd_ref) | copy-start | bytes 393220
  2.2 24.8 %all-to-all-start = ((bf16[32,64,128]{2,1,0:T(8,128)(2,1)}), bf16[32,64,128]{2,1,0:T(8,128)(2,1)S(1)}, u32[]{:S(2)}, u32[]{:S(2)}) async-start(bf16[32,64,128]{2,1,0:T(8,128)(2,1)} %pack.1), calls=%async_computation | async-start | bytes 1048576 | tf_op jit(solution)/shard_map/all_to_all | solution.py:138
  12.8 33.2 %collective-permute-start.1 = (bf16[1024,512]{1,0:T(8,128)(2,1)S(1)}, bf16[1024,512]{1,0:T(8,128)(2,1)S(1)}, u32[]{:S(2)}, u32[]{:S(2)}) collective-permute-start(bf16[1024,512]{1,0:T(8,128)(2,1)S(1)} %copy-done.2), channel_id=1, source_target_pairs={{0,14},{2,4},{4,2},{6,8},{8,6},{10,12},{12,10},{14,0},{1,15},{3,5}... | collective-permute-start | bytes 3145736 | tf_op jit(solution)/shard_map/ppermute | solution.py:133
  32.8 17.2 %all-to-all-start.1 = ((bf16[32,32,128]{2,1,0:T(8,128)(2,1)}), bf16[32,32,128]{2,1,0:T(8,128)(2,1)S(1)}, u32[]{:S(2)}, u32[]{:S(2)}) async-start(bf16[32,32,128]{2,1,0:T(8,128)(2,1)} %conv.1), calls=%async_computation.1 | async-start | bytes 524288 | tf_op jit(solution)/shard_map/all_to_all | solution.py:150
  50.0 0.7 copy-start.3
  59.4 20.3 %collective-permute-start = (bf16[2,128,1024]{2,1,0:T(8,128)(2,1)S(1)}, bf16[2,128,1024]{2,1,0:T(8,128)(2,1)S(1)}, u32[]{:S(2)}, u32[]{:S(2)}) collective-permute-start(bf16[2,128,1024]{2,1,0:T(8,128)(2,1)S(1)} %bitcast.22), channel_id=1, source_target_pairs={{0,12},{2,6},{4,0},{6,10},{8,4},{10,14},{12,8},{14,2},{1,13},{3,7}... | collective-permute-start | bytes 1572872 | tf_op jit(solution)/shard_map/ppermute | solution.py:165
  77.8 13.5 %collective-permute-start.2 = (bf16[256,256]{1,0:T(8,128)(2,1)S(1)}, bf16[256,256]{1,0:T(8,128)(2,1)S(1)}, u32[]{:S(2)}, u32[]{:S(2)}) collective-permute-start(bf16[256,256]{1,0:T(8,128)(2,1)S(1)} %get-tuple-element.15), channel_id=1, source_target_pairs={{0,14},{2,4},{4,2},{6,8},{8,6},{10,12},{12,10},{14,0},{1,15},{3,5}... | collective-permute-start | bytes 393224 | tf_op jit(solution)/shard_map/ppermute | solution.py:171
  85.6 8.6 %collective-permute-start.3 = (bf16[256,256]{1,0:T(8,128)(2,1)S(1)}, bf16[256,256]{1,0:T(8,128)(2,1)S(1)}, u32[]{:S(2)}, u32[]{:S(2)}) collective-permute-start(bf16[256,256]{1,0:T(8,128)(2,1)S(1)} %get-tuple-element.13), channel_id=1, source_target_pairs={{0,14},{2,4},{4,2},{6,8},{8,6},{10,12},{12,10},{14,0},{1,15},{3,5}... | collective-permute-start | bytes 393224 | tf_op jit(solution)/shard_map/ppermute | solution.py:171
  91.2 0.7 copy-start.4

commit v2 on v1

--- a/solution.py
+++ b/solution.py
@@ -26,12 +26,17 @@
     return np.concatenate(two_parts(forward), axis=0), np.stack(two_parts(inverse))
 
 
-def pack_kernel(values_ref, taps_ref, out_ref):
+def pack_kernel(values_ref, taps_ref, out_ref, values, taps, arrived):
     peers, rows, block = out_ref.shape
     width = rows // 2
-    for first, source in ((0, values_ref), (width, taps_ref)):
-        turned = source[...].astype(F32).T.astype(BF16)
-        out_ref[:, first : first + width, :] = turned.reshape(peers, width, block)
+    parts = ((0, values_ref, values), (1, taps_ref, taps))
+    copies = [pltpu.make_async_copy(source, here, arrived.at[n]) for n, source, here in parts]
+    for copy in copies:
+        copy.start()
+    for n, _, here in parts:
+        copies[n].wait()
+        turned = here[...].astype(F32).T.astype(BF16)
+        out_ref[:, n * width : (n + 1) * width, :] = turned.reshape(peers, width, block)
 
 
 def conv_kernel(in_ref, fwd_ref, inv_ref, out_ref, src, lag, spec):
@@ -69,7 +74,7 @@
                 spec[i0 + di, here, block:] = ss - rr - ii
         return carry
 
-    lax.fori_loop(0, width // 8, some_channels, 0)
+    lax.fori_loop(0, width // 8, some_channels, 0, unroll=True)
     whole = spec[...].reshape(count * width, 2 * block)
     high = whole.astype(BF16)
     low = (whole - high.astype(F32)).astype(BF16)
@@ -114,6 +119,7 @@
         place_kernel,
         in_specs=[pl.BlockSpec(memory_space=pltpu.SMEM)] + [pl.BlockSpec(memory_space=pltpu.VMEM)] * 3,
         out_shape=jax.ShapeDtypeStruct((seqs, block, own_a.shape[1]), BF16),
+        compiler_params=pltpu.CompilerParams(vmem_limit_bytes=4 * 2**20),
         name="place",
     )(place, own_a, own_b, got_a)
 
@@ -124,6 +130,7 @@
     width = chans // peers
     values, gates = values[0], gates[0]
     forward, inverse = dft_tables(block)
+    small = pltpu.CompilerParams(vmem_limit_bytes=8 * 2**20)
     count = lax.axis_size("rep")
     mine, core = lax.axis_index("rep"), lax.axis_index("fsdp")
     place = jnp.stack([mine, core]).astype(jnp.int32)
@@ -133,7 +140,16 @@
     partner_weight = lax.ppermute(out_weight, "rep", column_swap)
 
     packed = pl.pallas_call(
-        pack_kernel, out_shape=jax.ShapeDtypeStruct((peers, 2 * width, block), BF16), name="pack"
+        pack_kernel,
+        in_specs=[pl.BlockSpec(memory_space=pl.ANY)] * 2,
+        out_shape=jax.ShapeDtypeStruct((peers, 2 * width, block), BF16),
+        scratch_shapes=[
+            pltpu.VMEM(values.shape, BF16),
+            pltpu.VMEM(filter_taps.shape, F32),
+            pltpu.SemaphoreType.DMA((2,)),
+        ],
+        compiler_params=pltpu.CompilerParams(vmem_limit_bytes=60 * 2**20),
+        name="pack",
     )(values, filter_taps)
     turned = lax.all_to_all(packed, "ctx", split_axis=0, concat_axis=0, tiled=True)
     convolved = pl.pallas_call(
@@ -144,12 +160,15 @@
             pltpu.VMEM((3, peers, width, block), F32),
             pltpu.VMEM((peers, width, 2 * block), F32),
         ],
-        compiler_params=pltpu.CompilerParams(vmem_limit_bytes=40 * 2**20),
+        compiler_params=pltpu.CompilerParams(vmem_limit_bytes=20 * 2**20),
         name="conv",
     )(turned, forward, inverse)
     back = lax.all_to_all(convolved, "ctx", split_axis=0, concat_axis=0, tiled=True)
     mixed = pl.pallas_call(
-        gate_kernel, out_shape=jax.ShapeDtypeStruct((block, chans), BF16), name="gate"
+        gate_kernel,
+        out_shape=jax.ShapeDtypeStruct((block, chans), BF16),
+        compiler_params=small,
+        name="gate",
     )(back, values, gates, skip_gain[None, :])
 
     keep = out_weight.shape[1] // 2

time: 96 us -> 90.7 us (0.945)
  Pallas kernels: 11.8 us -> 7.47 us
  local copies, waits for them, and re-layouts: 3.58 us -> 2.54 us
  blocking collectives: 18 us -> 19 us
    all_to_all x1, waiting for transfers between devices: 3.91 us -> 1.13 us  [body(): lax.all_to_all(convolved, 'ctx', split_axis=0, concat_axis=0, tiled=True)]
    pallas_call x1, Pallas kernels: 5.74 us -> 3.77 us  [body(): pl.pallas_call(conv_kernel, out_shape=jax.ShapeDtypeStruct((peers, width,...]
    pallas_call x1, Pallas kernels: 1.95 us -> 0.15 us  [body(): pl.pallas_call(gate_kernel, out_shape=jax.ShapeDtypeStruct((block, chans)...]
    ppermute x2, waiting for transfers between devices: 0.36 us -> 2.07 us  [columns(): return (total[:, :keep], lax.ppermute(total[:, keep:], 'rep', column_swap))]
    dynamic_slice x2, local copies, waits for them, and re-layouts: 0.14 us -> 1.74 us  [body(): lax.dynamic_slice_in_dim(w, side * keep, keep, 1)]
    unnamed x10 -> x16, local copies, waits for them, and re-layouts: 1.37 us -> 0.03 us
    slice x2, local copies, waits for them, and re-layouts: 1.33 us -> 0.04 us  [columns(): return (total[:, :keep], lax.ppermute(total[:, keep:], 'rep', column_swap))]
    all_gather x2, blocking collectives: 11.3 us -> 12.5 us  [columns(): came = lax.all_gather(product[:, 2 * keep:].astype(BF16), 'fsdp', axis=0)]
  transfers between devices with their start and end apart: 6 -> 6, of which waited for: 4 -> 4; matrix products, arithmetic and copies ran while one was open for 4% -> 4% of each run, Pallas kernels for 8% -> 6%
where the time goes in v2:
time: 90.7 us; the launch traced here: 90.1 us
  starting transfers between devices  45.6 us (50%)
  blocking collectives  19 us (21%)
  waiting for transfers between devices  13.6 us (15%)
  Pallas kernels  7.47 us (8%)
  local copies, waits for them, and re-layouts  2.54 us (3%)
  matrix products  1.43 us (2%)
    all_gather x2, blocking collectives, columns(): came = lax.all_gather(product[:, 2 * keep:].astype(BF16), 'fsdp', axis=0)  12.5 us
    ppermute x1, starting transfers between devices, body(): partner_weight = lax.ppermute(out_weight, 'rep', column_swap)  10.7 us
    all_to_all x1, starting transfers between devices, body(): lax.all_to_all(packed, 'ctx', split_axis=0, concat_axis=0, tiled=True)  10.5 us
    ppermute x1, starting transfers between devices, body(): far = lax.ppermute(near, 'rep', onward)  10 us
    all_to_all x1, starting transfers between devices, body(): lax.all_to_all(convolved, 'ctx', split_axis=0, concat_axis=0, tiled=True)  7.47 us
    ppermute x2, starting transfers between devices, columns(): return (total[:, :keep], lax.ppermute(total[:, keep:], 'rep', column_swap))  6.93 us
    ppermute x1, waiting for transfers between devices, body(): partner_weight = lax.ppermute(out_weight, 'rep', column_swap)  6.78 us
    all_gather x1, blocking collectives, body(): near = lax.all_gather(mixed, 'rep', axis=0, axis_index_groups=row_pairs)  6.5 us
  transfers between devices with their start and end apart: 6, of which 4 were waited for; matrix products, arithmetic and copies ran while one was open for 4% of the time, Pallas kernels for 6%

profile of v2, /device:TPU:1, one launch (start us, length us, event | category | flops | bytes accessed | tf_op | source)
XLA Modules:
  0.0 90.1 jit_solution(12414385902608957536)
XLA Ops:
  0.0 2.2 %pack.1 = bf16[32,64,128]{2,1,0:T(8,128)(2,1)} custom-call(bf16[128,1024]{1,0:T(8,128)(2,1)} %bitcast.18, f32[128,1024]{1,0:T(8,128)} %taps_ref.1), custom_call_target="tpu_custom_call" | custom-call | tf_op jit(solution)/shard_map/pack/pallas_call | solution.py:142
  2.2 10.5 %all-to-all-start = ((bf16[32,64,128]{2,1,0:T(8,128)(2,1)}), bf16[32,64,128]{2,1,0:T(8,128)(2,1)S(1)}, u32[]{:S(2)}, u32[]{:S(2)}) async-start(bf16[32,64,128]{2,1,0:T(8,128)(2,1)} %pack.1), calls=%async_computation | async-start | bytes 1048576 | tf_op jit(solution)/shard_map/all_to_all | solution.py:154
  12.7 0.0 copy-done.5
  12.7 10.7 %collective-permute-start.1 = (bf16[1024,512]{1,0:T(8,128)(2,1)S(1)}, bf16[1024,512]{1,0:T(8,128)(2,1)S(1)}, u32[]{:S(2)}, u32[]{:S(2)}) collective-permute-start(bf16[1024,512]{1,0:T(8,128)(2,1)S(1)} %copy-done.5), channel_id=1, source_target_pairs={{0,14},{2,4},{4,2},{6,8},{8,6},{10,12},{12,10},{14,0},{1,15},{3,5}... | collective-permute-start | bytes 3145736 | tf_op jit(solution)/shard_map/ppermute | solution.py:140
  23.4 3.6 %all-to-all-done.in_ref = bf16[32,64,128]{2,1,0:T(8,128)(2,1)S(1)} async-done(((bf16[32,64,128]{2,1,0:T(8,128)(2,1)}), bf16[32,64,128]{2,1,0:T(8,128)(2,1)S(1)}, u32[]{:S(2)}, u32[]{:S(2)}) %all-to-all-start) | async-done | bytes 524320 | tf_op jit(solution)/shard_map/all_to_all | solution.py:154
  27.0 0.0 copy-done.2
  27.0 0.0 copy-done.3
  27.0 3.8 %conv.1 = bf16[32,32,128]{2,1,0:T(8,128)(2,1)} custom-call(bf16[32,64,128]{2,1,0:T(8,128)(2,1)S(1)} %all-to-all-done.in_ref, bf16[256,256]{1,0:T(8,128)(2,1)S(1)} %copy-done.3, bf16[2,256,256]{2,1,0:T(8,128)(2,1)S(1)} %copy-done.2), custom_call_target="tpu_custom_call" | custom-call | tf_op jit(solution)/shard_map/conv/pallas_call | solution.py:155
  30.8 7.5 %all-to-all-start.1 = ((bf16[32,32,128]{2,1,0:T(8,128)(2,1)}), bf16[32,32,128]{2,1,0:T(8,128)(2,1)S(1)}, u32[]{:S(2)}, u32[]{:S(2)}) async-start(bf16[32,32,128]{2,1,0:T(8,128)(2,1)} %conv.1), calls=%async_computation.1 | async-start | bytes 524288 | tf_op jit(solution)/shard_map/all_to_all | solution.py:166
  38.3 0.9 constant_dynamic-slice_fusion.3
  39.2 6.8 %collective-permute-done.1 = bf16[1024,512]{1,0:T(8,128)(2,1)S(1)} collective-permute-done((bf16[1024,512]{1,0:T(8,128)(2,1)S(1)}, bf16[1024,512]{1,0:T(8,128)(2,1)S(1)}, u32[]{:S(2)}, u32[]{:S(2)}) %collective-permute-start.1) | collective-permute-done | bytes 1048608 | tf_op jit(solution)/shard_map/ppermute | solution.py:140
  46.0 0.9 constant_dynamic-slice_fusion.2
  46.8 1.1 %all-to-all-done.1.conv_ref = bf16[32,32,128]{2,1,0:T(8,128)(2,1)S(1)} async-done(((bf16[32,32,128]{2,1,0:T(8,128)(2,1)}), bf16[32,32,128]{2,1,0:T(8,128)(2,1)S(1)}, u32[]{:S(2)}, u32[]{:S(2)}) %all-to-all-start.1) | async-done | bytes 262176 | tf_op jit(solution)/shard_map/all_to_all | solution.py:166
  48.0 0.0 copy-done
  48.0 0.0 copy-done.1
  48.0 0.1 gate.1
  48.1 6.5 %all-gather = bf16[256,1024]{1,0:T(8,128)(2,1)S(1)} all-gather(bf16[128,1024]{1,0:T(8,128)(2,1)S(1)} %gate.1), channel_id=2, replica_groups={{0,2},{4,6},{8,10},{12,14},{1,3},{5,7},{9,11},{13,15},{16,18},{20,22},{..., dimensions={0}, use_global_device_ids=true | all-gather | bytes 786432 | tf_op jit(solution)/shard_map/all_gather | solution.py:183
  54.6 10.0 %collective-permute-start = (bf16[2,128,1024]{2,1,0:T(8,128)(2,1)S(1)}, bf16[2,128,1024]{2,1,0:T(8,128)(2,1)S(1)}, u32[]{:S(2)}, u32[]{:S(2)}) collective-permute-start(bf16[2,128,1024]{2,1,0:T(8,128)(2,1)S(1)} %bitcast.24), channel_id=1, source_target_pairs={{0,12},{2,6},{4,0},{6,10},{8,4},{10,14},{12,8},{14,2},{1,13},{3,7}... | collective-permute-start | bytes 1572872 | tf_op jit(solution)/shard_map/ppermute | solution.py:184
  64.7 0.7 fusion.3
  65.4 6.9 %all-gather.1 = bf16[512,512]{1,0:T(8,128)(2,1)S(1)} all-gather(bf16[256,512]{1,0:T(8,128)(2,1)S(1)} %slice.51), channel_id=3, replica_groups=mesh['ctx'=32,'rep'=8,'fsdp'=2] {'fsdp'}, dimensions={0}, use_global_device_ids=true | all-gather | bytes 786432 | tf_op jit(solution)/shard_map/all_gather | solution.py:187
  72.4 0.1 fusion.1
  72.5 1.9 %collective-permute-start.2 = (bf16[256,256]{1,0:T(8,128)(2,1)S(1)}, bf16[256,256]{1,0:T(8,128)(2,1)S(1)}, u32[]{:S(2)}, u32[]{:S(2)}) collective-permute-start(bf16[256,256]{1,0:T(8,128)(2,1)S(1)} %get-tuple-element.15), channel_id=1, source_target_pairs={{0,14},{2,4},{4,2},{6,8},{8,6},{10,12},{12,10},{14,0},{1,15},{3,5}... | collective-permute-start | bytes 393224 | tf_op jit(solution)/shard_map/ppermute | solution.py:190
  74.4 0.0 collective-permute-done
  74.4 0.7 fusion.2
  75.2 5.6 %all-gather.2 = bf16[512,512]{1,0:T(8,128)(2,1)S(1)} all-gather(bf16[256,512]{1,0:T(8,128)(2,1)S(1)} %slice.50), channel_id=4, replica_groups=mesh['ctx'=32,'rep'=8,'fsdp'=2] {'fsdp'}, dimensions={0}, use_global_device_ids=true | all-gather | bytes 786432 | tf_op jit(solution)/shard_map/all_gather | solution.py:187
  80.7 0.1 fusion
  80.9 5.0 %collective-permute-start.3 = (bf16[256,256]{1,0:T(8,128)(2,1)S(1)}, bf16[256,256]{1,0:T(8,128)(2,1)S(1)}, u32[]{:S(2)}, u32[]{:S(2)}) collective-permute-start(bf16[256,256]{1,0:T(8,128)(2,1)S(1)} %get-tuple-element.13), channel_id=1, source_target_pairs={{0,14},{2,4},{4,2},{6,8},{8,6},{10,12},{12,10},{14,0},{1,15},{3,5}... | collective-permute-start | bytes 393224 | tf_op jit(solution)/shard_map/ppermute | solution.py:190
  85.9 0.1 pad_add_fusion.place_ref
  86.0 0.0 collective-permute-done.2.got_a
  86.0 1.4 %place.1 = bf16[8,128,256]{2,1,0:T(8,128)(2,1)} custom-call(s32[2]{0:T(128)S(1)} %pad_add_fusion.place_ref, bf16[256,256]{1,0:T(8,128)(2,1)S(1)} %get-tuple-element.7.own_a, bf16[256,256]{1,0:T(8,128)(2,1)S(1)} %get-tuple-element.14.own_b, bf16[256,256]{1,0:T(8,128)(2,1)S(1)} %collective-permute-done.2.got_a), custom_call_target="tpu_custom_call" | custom-call | tf_op jit(solution)/shard_map/place/pallas_call | solution.py:118
  87.4 2.1 %collective-permute-done.3 = bf16[256,256]{1,0:T(8,128)(2,1)S(1)} collective-permute-done((bf16[256,256]{1,0:T(8,128)(2,1)S(1)}, bf16[256,256]{1,0:T(8,128)(2,1)S(1)}, u32[]{:S(2)}, u32[]{:S(2)}) %collective-permute-start.3) | collective-permute-done | bytes 131104 | tf_op jit(solution)/shard_map/ppermute | solution.py:190
  89.4 0.7 constant_dynamic-update-slice_fusion
  (15 shorter events, 0.1 us)
Async XLA Ops:
  0.0 12.7 %copy-start.5 = (bf16[1024,512]{1,0:T(8,128)(2,1)S(1)}, bf16[1024,512]{1,0:T(8,128)(2,1)}, u32[]{:S(2)}) copy-start(bf16[1024,512]{1,0:T(8,128)(2,1)} %param.11) | copy-start | bytes 3145732
  0.0 27.0 %copy-start.2 = (bf16[2,256,256]{2,1,0:T(8,128)(2,1)S(1)}, bf16[2,256,256]{2,1,0:T(8,128)(2,1)}, u32[]{:S(2)}) copy-start(bf16[2,256,256]{2,1,0:T(8,128)(2,1)} %constant.55.clone.inv_ref) | copy-start | bytes 786436
  0.0 27.0 %copy-start.3 = (bf16[256,256]{1,0:T(8,128)(2,1)S(1)}, bf16[256,256]{1,0:T(8,128)(2,1)}, u32[]{:S(2)}) copy-start(bf16[256,256]{1,0:T(8,128)(2,1)} %constant.54.clone.fwd_ref) | copy-start | bytes 393220
  2.2 24.8 %all-to-all-start = ((bf16[32,64,128]{2,1,0:T(8,128)(2,1)}), bf16[32,64,128]{2,1,0:T(8,128)(2,1)S(1)}, u32[]{:S(2)}, u32[]{:S(2)}) async-start(bf16[32,64,128]{2,1,0:T(8,128)(2,1)} %pack.1), calls=%async_computation | async-start | bytes 1048576 | tf_op jit(solution)/shard_map/all_to_all | solution.py:154
  12.7 33.2 %collective-permute-start.1 = (bf16[1024,512]{1,0:T(8,128)(2,1)S(1)}, bf16[1024,512]{1,0:T(8,128)(2,1)S(1)}, u32[]{:S(2)}, u32[]{:S(2)}) collective-permute-start(bf16[1024,512]{1,0:T(8,128)(2,1)S(1)} %copy-done.5), channel_id=1, source_target_pairs={{0,14},{2,4},{4,2},{6,8},{8,6},{10,12},{12,10},{14,0},{1,15},{3,5}... | collective-permute-start | bytes 3145736 | tf_op jit(solution)/shard_map/ppermute | solution.py:140
  30.8 17.1 %all-to-all-start.1 = ((bf16[32,32,128]{2,1,0:T(8,128)(2,1)}), bf16[32,32,128]{2,1,0:T(8,128)(2,1)S(1)}, u32[]{:S(2)}, u32[]{:S(2)}) async-start(bf16[32,32,128]{2,1,0:T(8,128)(2,1)} %conv.1), calls=%async_computation.1 | async-start | bytes 524288 | tf_op jit(solution)/shard_map/all_to_all | solution.py:166
  39.2 8.8 %copy-start = (bf16[1,128,1024]{2,1,0:T(8,128)(2,1)S(1)}, bf16[1,128,1024]{2,1,0:T(8,128)(2,1)}, u32[]{:S(2)}) copy-start(bf16[1,128,1024]{2,1,0:T(8,128)(2,1)} %param.7) | copy-start | bytes 786436
  39.2 8.8 %copy-start.1 = (bf16[1,128,1024]{2,1,0:T(8,128)(2,1)S(1)}, bf16[1,128,1024]{2,1,0:T(8,128)(2,1)}, u32[]{:S(2)}) copy-start(bf16[1,128,1024]{2,1,0:T(8,128)(2,1)} %param.8) | copy-start | bytes 786436
  39.2 8.8 %copy-start.4 = (f32[1024]{0:T(1024)S(1)}, f32[1024]{0:T(1024)}, u32[]{:S(2)}) copy-start(f32[1024]{0:T(1024)} %param.9) | copy-start | bytes 12292
  46.8 17.8 %copy-start.6 = (bf16[1024,256]{1,0:T(8,128)(2,1)S(1)}, bf16[1024,256]{1,0:T(8,128)(2,1)}, u32[]{:S(2)}) copy-start(bf16[1024,256]{1,0:T(8,128)(2,1)} %get-tuple-element.10) | copy-start | bytes 1572868
  46.8 17.8 %copy-start.7 = (bf16[1024,256]{1,0:T(8,128)(2,1)S(1)}, bf16[1024,256]{1,0:T(8,128)(2,1)}, u32[]{:S(2)}) copy-start(bf16[1024,256]{1,0:T(8,128)(2,1)} %get-tuple-element.12) | copy-start | bytes 1572868
  54.6 19.8 %collective-permute-start = (bf16[2,128,1024]{2,1,0:T(8,128)(2,1)S(1)}, bf16[2,128,1024]{2,1,0:T(8,128)(2,1)S(1)}, u32[]{:S(2)}, u32[]{:S(2)}) collective-permute-start(bf16[2,128,1024]{2,1,0:T(8,128)(2,1)S(1)} %bitcast.24), channel_id=1, source_target_pairs={{0,12},{2,6},{4,0},{6,10},{8,4},{10,14},{12,8},{14,2},{1,13},{3,7}... | collective-permute-start | bytes 1572872 | tf_op jit(solution)/shard_map/ppermute | solution.py:184
  72.5 13.5 %collective-permute-start.2 = (bf16[256,256]{1,0:T(8,128)(2,1)S(1)}, bf16[256,256]{1,0:T(8,128)(2,1)S(1)}, u32[]{:S(2)}, u32[]{:S(2)}) collective-permute-start(bf16[256,256]{1,0:T(8,128)(2,1)S(1)} %get-tuple-element.15), channel_id=1, source_target_pairs={{0,14},{2,4},{4,2},{6,8},{8,6},{10,12},{12,10},{14,0},{1,15},{3,5}... | collective-permute-start | bytes 393224 | tf_op jit(solution)/shard_map/ppermute | solution.py:190
  80.9 8.6 %collective-permute-start.3 = (bf16[256,256]{1,0:T(8,128)(2,1)S(1)}, bf16[256,256]{1,0:T(8,128)(2,1)S(1)}, u32[]{:S(2)}, u32[]{:S(2)}) collective-permute-start(bf16[256,256]{1,0:T(8,128)(2,1)S(1)} %get-tuple-element.13), channel_id=1, source_target_pairs={{0,14},{2,4},{4,2},{6,8},{8,6},{10,12},{12,10},{14,0},{1,15},{3,5}... | collective-permute-start | bytes 393224 | tf_op jit(solution)/shard_map/ppermute | solution.py:190

commit v3 on v2

--- a/solution.py
+++ b/solution.py
@@ -193,9 +193,17 @@
         jnp.dot(near.reshape(2 * block, chans), weights, preferred_element_type=F32)
     )
     far, own_a = lax.optimization_barrier((far, own_a))
-    own_b, got_b = columns(
-        jnp.dot(far.reshape(2 * block, chans), weights, preferred_element_type=F32)
-    )
+    far_rows = far.reshape(2 * block, chans)
+
+    def one_block(first):
+        here, away = (weights[:, at : at + keep] for at in (first, first + 2 * keep))
+        sent = jnp.dot(far_rows, away, preferred_element_type=F32).astype(BF16)
+        came = lax.all_gather(sent, "fsdp", axis=0)
+        kept = jnp.dot(far_rows, here, preferred_element_type=F32)
+        return (kept + lax.dynamic_index_in_dim(came, 1 - core, 0, False).astype(F32)).astype(BF16)
+
+    got_b = lax.ppermute(one_block(keep), "rep", column_swap)
+    own_b = one_block(0)
     out = place_most(place, own_a, own_b, got_a, count, block)
     low = jnp.where(mine % 2 == 1, mine + 3, mine - 4 + count) % count
     return lax.dynamic_update_slice(out, got_b.reshape(2, block, keep), (low, 0, 0))

time: 90.7 us -> 92.6 us (1.021)
  blocking collectives: 19 us -> 20.8 us
    all_gather x0 -> x2, blocking collectives: none -> 7.4 us  [one_block(): came = lax.all_gather(sent, 'fsdp', axis=0)]
    all_gather x2 -> x1, blocking collectives: 12.5 us -> 6.92 us  [columns(): came = lax.all_gather(product[:, 2 * keep:].astype(BF16), 'fsdp', axis=0)]
    ppermute x2 -> x1, starting transfers between devices: 6.93 us -> 1.92 us  [columns(): return (total[:, :keep], lax.ppermute(total[:, keep:], 'rep', column_swap))]
    ppermute x0 -> x1, starting transfers between devices: none -> 5 us  [body(): got_b = lax.ppermute(one_block(keep), 'rep', column_swap)]
    ppermute x2 -> x1, waiting for transfers between devices: 2.07 us -> 0.01 us  [columns(): return (total[:, :keep], lax.ppermute(total[:, keep:], 'rep', column_swap))]
    ppermute x0 -> x1, waiting for transfers between devices: none -> 1.86 us  [body(): got_b = lax.ppermute(one_block(keep), 'rep', column_swap)]
where the time goes in v3:
time: 92.6 us; the launch traced here: 92 us
  starting transfers between devices  45.6 us (49%)
  blocking collectives  20.8 us (22%)
  waiting for transfers between devices  13.7 us (15%)
  Pallas kernels  7.48 us (8%)
  local copies, waits for them, and re-layouts  2.08 us (2%)
  matrix products  1.94 us (2%)
    ppermute x1, starting transfers between devices, body(): partner_weight = lax.ppermute(out_weight, 'rep', column_swap)  10.7 us
    all_to_all x1, starting transfers between devices, body(): lax.all_to_all(packed, 'ctx', split_axis=0, concat_axis=0, tiled=True)  10.5 us
    ppermute x1, starting transfers between devices, body(): far = lax.ppermute(near, 'rep', onward)  10 us
    ppermute x1, waiting for transfers between devices, body(): partner_weight = lax.ppermute(out_weight, 'rep', column_swap)  7.53 us
    all_to_all x1, starting transfers between devices, body(): lax.all_to_all(convolved, 'ctx', split_axis=0, concat_axis=0, tiled=True)  7.49 us
    all_gather x2, blocking collectives, one_block(): came = lax.all_gather(sent, 'fsdp', axis=0)  7.4 us
    all_gather x1, blocking collectives, columns(): came = lax.all_gather(product[:, 2 * keep:].astype(BF16), 'fsdp', axis=0)  6.92 us
    all_gather x1, blocking collectives, body(): near = lax.all_gather(mixed, 'rep', axis=0, axis_index_groups=row_pairs)  6.48 us
  transfers between devices with their start and end apart: 6, of which 4 were waited for; matrix products, arithmetic and copies ran while one was open for 4% of the time, Pallas kernels for 6%

profile of v3, /device:TPU:1, one launch (start us, length us, event | category | flops | bytes accessed | tf_op | source)
XLA Modules:
  0.0 92.0 jit_solution(10012882874064471188)
XLA Ops:
  0.0 2.2 %pack.1 = bf16[32,64,128]{2,1,0:T(8,128)(2,1)} custom-call(bf16[128,1024]{1,0:T(8,128)(2,1)} %bitcast.29, f32[128,1024]{1,0:T(8,128)} %taps_ref.1), custom_call_target="tpu_custom_call" | custom-call | tf_op jit(solution)/shard_map/pack/pallas_call | solution.py:142
  2.2 10.5 %all-to-all-start = ((bf16[32,64,128]{2,1,0:T(8,128)(2,1)}), bf16[32,64,128]{2,1,0:T(8,128)(2,1)S(1)}, u32[]{:S(2)}, u32[]{:S(2)}) async-start(bf16[32,64,128]{2,1,0:T(8,128)(2,1)} %pack.1), calls=%async_computation | async-start | bytes 1048576 | tf_op jit(solution)/shard_map/all_to_all | solution.py:154
  12.7 10.7 %collective-permute-start.1 = (bf16[1024,512]{1,0:T(8,128)(2,1)S(1)}, bf16[1024,512]{1,0:T(8,128)(2,1)}, u32[]{:S(2)}, u32[]{:S(2)}) collective-permute-start(bf16[1024,512]{1,0:T(8,128)(2,1)S(1)} %copy-done.5), channel_id=1, source_target_pairs={{0,14},{2,4},{4,2},{6,8},{8,6},{10,12},{12,10},{14,0},{1,15},{3,5}... | collective-permute-start | bytes 3145736 | tf_op jit(solution)/shard_map/ppermute | solution.py:140
  23.4 3.6 %all-to-all-done.in_ref = bf16[32,64,128]{2,1,0:T(8,128)(2,1)S(1)} async-done(((bf16[32,64,128]{2,1,0:T(8,128)(2,1)}), bf16[32,64,128]{2,1,0:T(8,128)(2,1)S(1)}, u32[]{:S(2)}, u32[]{:S(2)}) %all-to-all-start) | async-done | bytes 524320 | tf_op jit(solution)/shard_map/all_to_all | solution.py:154
  27.0 3.8 %conv.1 = bf16[32,32,128]{2,1,0:T(8,128)(2,1)} custom-call(bf16[32,64,128]{2,1,0:T(8,128)(2,1)S(1)} %all-to-all-done.in_ref, bf16[256,256]{1,0:T(8,128)(2,1)S(1)} %copy-done.3, bf16[2,256,256]{2,1,0:T(8,128)(2,1)S(1)} %copy-done.2), custom_call_target="tpu_custom_call" | custom-call | tf_op jit(solution)/shard_map/conv/pallas_call | solution.py:155
  30.8 7.5 %all-to-all-start.1 = ((bf16[32,32,128]{2,1,0:T(8,128)(2,1)}), bf16[32,32,128]{2,1,0:T(8,128)(2,1)S(1)}, u32[]{:S(2)}, u32[]{:S(2)}) async-start(bf16[32,32,128]{2,1,0:T(8,128)(2,1)} %conv.1), calls=%async_computation.1 | async-start | bytes 524288 | tf_op jit(solution)/shard_map/all_to_all | solution.py:166
  38.3 0.1 pad_add_fusion.place_ref
  38.4 0.1 constant_dynamic-slice_fusion.3
  38.5 0.0 copy-start
  38.5 0.0 copy-start.1
  38.5 0.0 copy-start.4
  38.5 7.5 %collective-permute-done.1 = bf16[1024,512]{1,0:T(8,128)(2,1)} collective-permute-done((bf16[1024,512]{1,0:T(8,128)(2,1)S(1)}, bf16[1024,512]{1,0:T(8,128)(2,1)}, u32[]{:S(2)}, u32[]{:S(2)}) %collective-permute-start.1) | collective-permute-done | bytes 1048608 | tf_op jit(solution)/shard_map/ppermute | solution.py:140
  46.1 1.3 %constant_dynamic-slice_fusion.2 = (bf16[1024,256]{1,0:T(8,128)(2,1)S(1)}, bf16[1024,256]{1,0:T(8,128)(2,1)S(1)}) fusion(bf16[1024,512]{1,0:T(8,128)(2,1)} %collective-permute-done.1, s32[]{:T(128)S(6)} %select_n.32, s32[]{:T(128)S(6)} %select_n.33), kind=kLoop, calls=%fused_computation.20 | loop fusion | bytes 2097160 | tf_op jit(solution)/shard_map/dynamic_slice | solution.py:177
  47.3 0.6 all-to-all-done.1.conv_ref
  48.0 0.1 gate.1
  48.1 6.5 %all-gather = bf16[256,1024]{1,0:T(8,128)(2,1)S(1)} all-gather(bf16[128,1024]{1,0:T(8,128)(2,1)S(1)} %gate.1), channel_id=2, replica_groups={{0,2},{4,6},{8,10},{12,14},{1,3},{5,7},{9,11},{13,15},{16,18},{20,22},{..., dimensions={0}, use_global_device_ids=true | all-gather | bytes 786432 | tf_op jit(solution)/shard_map/all_gather | solution.py:183
  54.6 10.0 %collective-permute-start = (bf16[2,128,1024]{2,1,0:T(8,128)(2,1)S(1)}, bf16[2,128,1024]{2,1,0:T(8,128)(2,1)S(1)}, u32[]{:S(2)}, u32[]{:S(2)}) collective-permute-start(bf16[2,128,1024]{2,1,0:T(8,128)(2,1)S(1)} %bitcast.40), channel_id=1, source_target_pairs={{0,12},{2,6},{4,0},{6,10},{8,4},{10,14},{12,8},{14,2},{1,13},{3,7}... | collective-permute-start | bytes 1572872 | tf_op jit(solution)/shard_map/ppermute | solution.py:184
  64.7 0.7 fusion
  65.4 6.9 %all-gather.1 = bf16[512,512]{1,0:T(8,128)(2,1)S(1)} all-gather(bf16[256,512]{1,0:T(8,128)(2,1)S(1)} %slice.25), channel_id=3, replica_groups=mesh['ctx'=32,'rep'=8,'fsdp'=2] {'fsdp'}, dimensions={0}, use_global_device_ids=true | all-gather | bytes 786432 | tf_op jit(solution)/shard_map/all_gather | solution.py:187
  72.3 0.1 fusion.10
  72.5 1.9 %collective-permute-start.2 = (bf16[256,256]{1,0:T(8,128)(2,1)S(1)}, bf16[256,256]{1,0:T(8,128)(2,1)S(1)}, u32[]{:S(2)}, u32[]{:S(2)}) collective-permute-start(bf16[256,256]{1,0:T(8,128)(2,1)S(1)} %get-tuple-element.13), channel_id=1, source_target_pairs={{0,14},{2,4},{4,2},{6,8},{8,6},{10,12},{12,10},{14,0},{1,15},{3,5}... | collective-permute-start | bytes 393224 | tf_op jit(solution)/shard_map/ppermute | solution.py:190
  74.4 0.0 collective-permute-done
  74.4 0.3 convolution_convert_fusion
  74.7 0.3 convolution_convert_fusion.1
  75.0 5.4 %all-gather.2 = bf16[512,256]{1,0:T(8,128)(2,1)S(1)} all-gather(bf16[256,256]{1,0:T(8,128)(2,1)S(1)} %convolution_convert_fusion.1), channel_id=4, replica_groups=mesh['ctx'=32,'rep'=8,'fsdp'=2] {'fsdp'}, dimensions={0}, use_global_device_ids=true | all-gather | bytes 393216 | tf_op jit(solution)/shard_map/all_gather | solution.py:201
  80.4 2.0 %all-gather.3 = bf16[512,256]{1,0:T(8,128)(2,1)S(1)} all-gather(bf16[256,256]{1,0:T(8,128)(2,1)S(1)} %convolution_convert_fusion), channel_id=5, replica_groups=mesh['ctx'=32,'rep'=8,'fsdp'=2] {'fsdp'}, dimensions={0}, use_global_device_ids=true | all-gather | bytes 393216 | tf_op jit(solution)/shard_map/all_gather | solution.py:201
  82.4 0.3 fusion.9
  82.7 5.0 %collective-permute-start.3 = (bf16[256,256]{1,0:T(8,128)(2,1)S(1)}, bf16[256,256]{1,0:T(8,128)(2,1)S(1)}, u32[]{:S(2)}, u32[]{:S(2)}) collective-permute-start(bf16[256,256]{1,0:T(8,128)(2,1)S(1)} %fusion.9), channel_id=1, source_target_pairs={{0,14},{2,4},{4,2},{6,8},{8,6},{10,12},{12,10},{14,0},{1,15},{3,5}... | collective-permute-start | bytes 393224 | tf_op jit(solution)/shard_map/ppermute | solution.py:205
  87.7 0.3 fusion.8.own_b
  88.1 1.4 %place.1 = bf16[8,128,256]{2,1,0:T(8,128)(2,1)} custom-call(s32[2]{0:T(128)S(1)} %pad_add_fusion.place_ref, bf16[256,256]{1,0:T(8,128)(2,1)S(1)} %get-tuple-element.7.own_a, bf16[256,256]{1,0:T(8,128)(2,1)S(1)} %fusion.8.own_b, bf16[256,256]{1,0:T(8,128)(2,1)S(1)} %collective-permute-done.2.got_a), custom_call_target="tpu_custom_call" | custom-call | tf_op jit(solution)/shard_map/place/pallas_call | solution.py:118
  89.4 1.9 %collective-permute-done.3 = bf16[256,256]{1,0:T(8,128)(2,1)S(1)} collective-permute-done((bf16[256,256]{1,0:T(8,128)(2,1)S(1)}, bf16[256,256]{1,0:T(8,128)(2,1)S(1)}, u32[]{:S(2)}, u32[]{:S(2)}) %collective-permute-start.3) | collective-permute-done | bytes 131104 | tf_op jit(solution)/shard_map/ppermute | solution.py:205
  91.3 0.7 constant_dynamic-update-slice_fusion
  (12 shorter events, 0.1 us)
Async XLA Ops:
  0.0 12.7 %copy-start.5 = (bf16[1024,512]{1,0:T(8,128)(2,1)S(1)}, bf16[1024,512]{1,0:T(8,128)(2,1)}, u32[]{:S(2)}) copy-start(bf16[1024,512]{1,0:T(8,128)(2,1)} %param.11) | copy-start | bytes 3145732
  0.0 27.0 %copy-start.2 = (bf16[2,256,256]{2,1,0:T(8,128)(2,1)S(1)}, bf16[2,256,256]{2,1,0:T(8,128)(2,1)}, u32[]{:S(2)}) copy-start(bf16[2,256,256]{2,1,0:T(8,128)(2,1)} %constant.59.clone.inv_ref) | copy-start | bytes 786436
  0.0 27.0 %copy-start.3 = (bf16[256,256]{1,0:T(8,128)(2,1)S(1)}, bf16[256,256]{1,0:T(8,128)(2,1)}, u32[]{:S(2)}) copy-start(bf16[256,256]{1,0:T(8,128)(2,1)} %constant.58.clone.fwd_ref) | copy-start | bytes 393220
  2.2 24.8 %all-to-all-start = ((bf16[32,64,128]{2,1,0:T(8,128)(2,1)}), bf16[32,64,128]{2,1,0:T(8,128)(2,1)S(1)}, u32[]{:S(2)}, u32[]{:S(2)}) async-start(bf16[32,64,128]{2,1,0:T(8,128)(2,1)} %pack.1), calls=%async_computation | async-start | bytes 1048576 | tf_op jit(solution)/shard_map/all_to_all | solution.py:154
  12.7 33.3 %collective-permute-start.1 = (bf16[1024,512]{1,0:T(8,128)(2,1)S(1)}, bf16[1024,512]{1,0:T(8,128)(2,1)}, u32[]{:S(2)}, u32[]{:S(2)}) collective-permute-start(bf16[1024,512]{1,0:T(8,128)(2,1)S(1)} %copy-done.5), channel_id=1, source_target_pairs={{0,14},{2,4},{4,2},{6,8},{8,6},{10,12},{12,10},{14,0},{1,15},{3,5}... | collective-permute-start | bytes 3145736 | tf_op jit(solution)/shard_map/ppermute | solution.py:140
  30.8 17.2 %all-to-all-start.1 = ((bf16[32,32,128]{2,1,0:T(8,128)(2,1)}), bf16[32,32,128]{2,1,0:T(8,128)(2,1)S(1)}, u32[]{:S(2)}, u32[]{:S(2)}) async-start(bf16[32,32,128]{2,1,0:T(8,128)(2,1)} %conv.1), calls=%async_computation.1 | async-start | bytes 524288 | tf_op jit(solution)/shard_map/all_to_all | solution.py:166
  38.5 9.5 %copy-start = (bf16[1,128,1024]{2,1,0:T(8,128)(2,1)S(1)}, bf16[1,128,1024]{2,1,0:T(8,128)(2,1)}, u32[]{:S(2)}) copy-start(bf16[1,128,1024]{2,1,0:T(8,128)(2,1)} %param.7) | copy-start | bytes 786436
  38.5 9.5 %copy-start.1 = (bf16[1,128,1024]{2,1,0:T(8,128)(2,1)S(1)}, bf16[1,128,1024]{2,1,0:T(8,128)(2,1)}, u32[]{:S(2)}) copy-start(bf16[1,128,1024]{2,1,0:T(8,128)(2,1)} %param.8) | copy-start | bytes 786436
  38.5 9.5 %copy-start.4 = (f32[1024]{0:T(1024)S(1)}, f32[1024]{0:T(1024)}, u32[]{:S(2)}) copy-start(f32[1024]{0:T(1024)} %param.9) | copy-start | bytes 12292
  54.6 19.8 %collective-permute-start = (bf16[2,128,1024]{2,1,0:T(8,128)(2,1)S(1)}, bf16[2,128,1024]{2,1,0:T(8,128)(2,1)S(1)}, u32[]{:S(2)}, u32[]{:S(2)}) collective-permute-start(bf16[2,128,1024]{2,1,0:T(8,128)(2,1)S(1)} %bitcast.40), channel_id=1, source_target_pairs={{0,12},{2,6},{4,0},{6,10},{8,4},{10,14},{12,8},{14,2},{1,13},{3,7}... | collective-permute-start | bytes 1572872 | tf_op jit(solution)/shard_map/ppermute | solution.py:184
  72.5 15.6 %collective-permute-start.2 = (bf16[256,256]{1,0:T(8,128)(2,1)S(1)}, bf16[256,256]{1,0:T(8,128)(2,1)S(1)}, u32[]{:S(2)}, u32[]{:S(2)}) collective-permute-start(bf16[256,256]{1,0:T(8,128)(2,1)S(1)} %get-tuple-element.13), channel_id=1, source_target_pairs={{0,14},{2,4},{4,2},{6,8},{8,6},{10,12},{12,10},{14,0},{1,15},{3,5}... | collective-permute-start | bytes 393224 | tf_op jit(solution)/shard_map/ppermute | solution.py:190
  82.7 8.6 %collective-permute-start.3 = (bf16[256,256]{1,0:T(8,128)(2,1)S(1)}, bf16[256,256]{1,0:T(8,128)(2,1)S(1)}, u32[]{:S(2)}, u32[]{:S(2)}) collective-permute-start(bf16[256,256]{1,0:T(8,128)(2,1)S(1)} %fusion.9), channel_id=1, source_target_pairs={{0,14},{2,4},{4,2},{6,8},{8,6},{10,12},{12,10},{14,0},{1,15},{3,5}... | collective-permute-start | bytes 393224 | tf_op jit(solution)/shard_map/ppermute | solution.py:205
